TPU v7x, 512 devices: a whole 4x4x16 slice. The times are simulated.
512 devices in a mesh: half: 2 (over core), row: 16 (over z), col: 16 (over y, x).
Axes of the slice: x: 4, y: 4, z: 16, core: 2. Of those that a mesh axis runs over, the one named last changes fastest.
Arguments:
- child_front: float32 [2, 8192, 8192], P('half', 'row', 'col'), as said below
- child_map: int32 [2, 48], P('half'), may hold values from 0 to 63, as said below
- root_front: float32 [8192, 16, 2, 256], P('row', 'col', 'half'), as said below
Outputs:
- child_panel: float32 [2, 512, 8192], P('half', None, 'col')
- root_panel: float32 [512, 16, 2, 256], P(None, 'col', 'half')
- root_update: float32 [8192, 16, 2, 256], P('row', 'col', 'half')
Inputs may be any that keep to these rules, and one draw needn't show every extreme that they name: `child_map`: for child h, the update blocks of row part k (the 3 blocks after that part's first block) map in increasing order to distinct blocks among the root's blocks k * 4 to (k + 1) * 4 - 1. `child_front`: each child's front is symmetric and positive definite. `root_front`: the root front is symmetric and positive definite.
All inputs are finite; a program needn't handle non-finite values.
Results may differ from a plain program's by a relative error of at most 0.0001.
Values sent between devices are 32-bit elements; how exact they have to be, the bound alone decides.
A program may use at most 64 MiB of HBM per device.

v0:
```python
import jax
import jax.numpy as jnp
from jax import lax
from jax.sharding import PartitionSpec as P

BLK = 128
PB = 32


def spread_2(value, axis, source):
    kept = jnp.where(lax.axis_index(axis) == source, value, 0).astype(value.dtype)
    return lax.psum(kept, axis)


def lower_solve(factor, right):
    return lax.linalg.triangular_solve(factor, right, left_side=True, lower=True)


def transposed_product(left, right):
    return lax.dot_general(
        left,
        right,
        (((0,), (0,)), ((), ())),
        precision=lax.Precision.HIGHEST,
        preferred_element_type=jnp.float32,
    )


def selector(child_row_map, part_index, child_tiles, root_tiles):
    per_part = child_tiles - 1
    targets = (
        lax.dynamic_slice_in_dim(child_row_map, part_index * per_part, per_part)
        - part_index * root_tiles
    )
    one_hot = (jnp.arange(root_tiles, dtype=jnp.int32)[:, None] == targets[None, :]).astype(
        jnp.float32
    )
    return jnp.concatenate([jnp.zeros((root_tiles, 1), jnp.float32), one_hot], axis=1)


def body(child_front, child_map, root_front):
    tile_rows = BLK
    pivot_count = PB
    child_block = child_front[0]
    part_rows = child_block.shape[0]
    row_part = lax.axis_index("row")
    col_part = lax.axis_index("col")
    strips = lax.all_gather(child_block[:pivot_count, :], "row", axis=0, tiled=True)
    pieces = lax.all_gather(
        child_block[None, :pivot_count, :pivot_count], ("row", "col"), axis=0, tiled=True
    )
    parts_count = lax.axis_size("row")
    corner = pieces.reshape(parts_count, parts_count, pivot_count, pivot_count).transpose(
        0, 2, 1, 3
    )
    corner = corner.reshape(parts_count * pivot_count, parts_count * pivot_count)
    factor = jnp.linalg.cholesky(corner)
    child_panel = lower_solve(factor, strips)
    columns = lax.all_gather(child_block[:, :pivot_count], "col", axis=1, tiled=True)
    panel_rows = lower_solve(factor, columns.T)
    update = child_block - transposed_product(panel_rows, child_panel)
    root_rows = root_front.shape[0]
    child_tiles = part_rows // tile_rows
    root_tiles = root_rows // tile_rows
    own_map = child_map[0]
    row_select = selector(own_map, row_part, child_tiles, root_tiles)
    col_select = selector(own_map, col_part, child_tiles, root_tiles)
    blocks = update.reshape(child_tiles, tile_rows, child_tiles, tile_rows)
    spread = jnp.einsum("ap,piqj->aiqj", row_select, blocks, precision=lax.Precision.HIGHEST)
    spread = jnp.einsum("aiqj,bq->aibj", spread, col_select, precision=lax.Precision.HIGHEST)
    additions = spread.reshape(root_rows, 2, root_rows // 2)
    joined = lax.psum_scatter(additions, "half", scatter_dimension=1, tiled=True)
    assembled = root_front[:, 0, 0, :] + joined[:, 0, :]
    root_strips = lax.all_gather(assembled[:pivot_count, :], "row", axis=0, tiled=True)
    pivots = spread_2(root_strips[:, :pivot_count], "half", 0)
    root_corner = lax.all_gather(pivots, "col", axis=1, tiled=True)
    root_factor = jnp.linalg.cholesky(root_corner)
    root_panel = lower_solve(root_factor, root_strips)
    mirrored = spread_2(root_panel, "col", row_part)
    both_halves = lax.all_gather(mirrored[:, None, :], "half", axis=1, tiled=True)
    panel_side = both_halves.reshape(both_halves.shape[0], root_rows)
    root_update = assembled - transposed_product(panel_side, root_panel)
    return (child_panel[None], root_panel[:, None, None, :], root_update[:, None, None, :])


def solution(mesh):
    return jax.shard_map(
        body,
        mesh=mesh,
        in_specs=(P("half", "row", "col"), P("half", None), P("row", "col", "half", None)),
        out_specs=(
            P("half", None, "col"),
            P(None, "col", "half", None),
            P("row", "col", "half", None),
        ),
        check_vma=False,
    )
```

profile of v0, /device:TPU:1, one launch (start us, length us, event | category | flops | bytes accessed | tf_op | source)
XLA Modules:
  0.0 844.2 jit_solution(4435899986150828886)
XLA Ops:
  10.4 1.5 slice.132
  12.8 208.7 %all-gather.14.cloned.1.call-done = f32[8192,32]{1,0:T(8,128)} async-done(((f32[32,32]{1,0:T(8,128)}), f32[8192,32]{1,0:T(8,128)}) %all-gather.14.cloned.1.call-update) | async-done | bytes 1048592 | tf_op jit(solution)/shard_map/all_gather | solution.py:49
  221.5 5.6 copy.23
  227.1 3.5 reshape.68
  232.2 11.7 %cholesky.286 = f32[128,128]{1,0:T(8,128)S(1)} custom-call(f32[128,128]{1,0:T(8,128)S(1)} %cholesky.426), custom_call_target="Cholesky" | custom-call | tf_op jit(solution)/shard_map/jit(cholesky)/cholesky | solution.py:57
  244.0 9.8 %custom-call.31 = f32[1,128,128]{1,2,0:T(8,128)S(1)} custom-call(f32[1,128,128]{2,1,0:T(8,128)S(1)} %get-tuple-element.79), custom_call_target="InvertDiagBlocksLowerTriangular" | custom-call | tf_op jit(solution)/shard_map/jit(cholesky)/cholesky | solution.py:57
  256.4 11.7 %cholesky.305 = f32[128,128]{1,0:T(8,128)S(1)} custom-call(f32[128,128]{1,0:T(8,128)S(1)} %cholesky.430), custom_call_target="Cholesky" | custom-call | tf_op jit(solution)/shard_map/jit(cholesky)/cholesky | solution.py:57
  268.2 10.0 %custom-call.32 = f32[1,128,128]{1,2,0:T(8,128)S(1)} custom-call(f32[1,128,128]{2,1,0:T(8,128)S(1)} %get-tuple-element.76), custom_call_target="InvertDiagBlocksLowerTriangular" | custom-call | tf_op jit(solution)/shard_map/jit(cholesky)/cholesky | solution.py:57
  279.7 11.7 %cholesky.326 = f32[128,128]{1,0:T(8,128)S(1)} custom-call(f32[128,128]{1,0:T(8,128)S(1)} %cholesky.435), custom_call_target="Cholesky" | custom-call | tf_op jit(solution)/shard_map/jit(cholesky)/cholesky | solution.py:57
  292.2 9.8 %custom-call.33 = f32[1,128,128]{1,2,0:T(8,128)S(1)} custom-call(f32[1,128,128]{2,1,0:T(8,128)S(1)} %get-tuple-element.73), custom_call_target="InvertDiagBlocksLowerTriangular" | custom-call | tf_op jit(solution)/shard_map/jit(cholesky)/cholesky | solution.py:57
  303.5 11.7 %cholesky.343 = f32[128,128]{1,0:T(8,128)S(1)} custom-call(f32[128,128]{1,0:T(8,128)S(1)} %convolution_subtract_fusion.16), custom_call_target="Cholesky" | custom-call | tf_op jit(solution)/shard_map/jit(cholesky)/cholesky | solution.py:57
  319.6 8.5 %while.6 = (s32[]{:T(128)}, f32[512,512]{1,0:T(8,128)S(1)}, s32[4,2]{0,1:T(2,128)S(1)}, f32[4,128,128]{2,1,0:T(8,128)S(1)}, s32[]{:T(128)}) while((s32[]{:T(128)}, f32[512,512]{1,0:T(8,128)S(1)}, s32[4,2]{0,1:T(2,128)S(1)}, f32[4,128,128]{2,1,0:T(8,128)S(1)}, s32[]{:T(128)}) %tuple.64), condition=%wide.while_cond, body=%wide.while_body.sunk | while | flops 2 | bytes 131181 | solution.py:16
  320.3 1.4 bitcast_dynamic-update-slice_fusion.5
  322.4 1.4 bitcast_dynamic-update-slice_fusion.5
  324.6 1.4 bitcast_dynamic-update-slice_fusion.5
  326.7 1.4 bitcast_dynamic-update-slice_fusion.5
  328.1 39.3 %custom-call.34 = f32[4,128,128]{1,2,0:T(8,128)S(1)} custom-call(f32[4,128,128]{2,1,0:T(8,128)S(1)} %get-tuple-element.27), custom_call_target="InvertDiagBlocksLowerTriangular" | custom-call | tf_op jit(solution)/shard_map/triangular_solve/custom-call.3 | solution.py:16
  367.5 1.4 fusion.36
  373.1 1.6 convolution_subtract_fusion.6
  375.8 1.4 fusion.38
  379.0 1.4 convolution_subtract_fusion.4
  380.8 1.6 convolution_subtract_fusion.7
  383.6 3.1 convolution_subtract_fusion
  387.0 1.7 fusion.11
  392.0 23.3 %reduce-scatter.2.cloned.1.call-done = f32[512,1,256]{2,0,1:T(8,128)} async-done(((f32[512,2,256]{2,0,1:T(8,128)}), f32[512,1,256]{2,0,1:T(8,128)}) %reduce-scatter.2.cloned.1.call-update) | async-done | bytes 524304 | tf_op jit(solution)/shard_map/reduce_scatter | solution.py:72
  417.2 25.4 %all_gather.21 = f32[512,256]{1,0:T(8,128)S(1)} all-gather(f32[32,256]{1,0:T(8,128)S(1)} %slice.211), channel_id=1, replica_groups=mesh['half'=2,'row'=16,'col'=16] {'row'}, dimensions={0}, use_global_device_ids=true | all-gather | bytes 557056 | tf_op jit(solution)/shard_map/all_gather | solution.py:74
  443.4 44.3 %all-reduce.6.cloned.1.call-done = f32[512,32]{0,1:T(8,128)} async-done(((f32[512,32]{0,1:T(8,128)}), f32[512,32]{0,1:T(8,128)}) %all-reduce.6.cloned.1.call-update) | async-done | bytes 65552 | tf_op jit(solution)/shard_map/psum | solution.py:12
  487.9 59.6 %all-gather.10.cloned.1.call-done = f32[512,512]{0,1:T(8,128)} async-done(((f32[512,32]{0,1:T(8,128)}), f32[512,512]{0,1:T(8,128)}) %all-gather.10.cloned.1.call-update) | async-done | bytes 1048592 | tf_op jit(solution)/shard_map/all_gather | solution.py:76
  547.5 1.6 copy.30
  549.1 1.4 fusion.8
  550.5 11.7 %cholesky.358 = f32[128,128]{1,0:T(8,128)S(1)} custom-call(f32[128,128]{1,0:T(8,128)S(1)} %cholesky.439), custom_call_target="Cholesky" | custom-call | tf_op jit(solution)/shard_map/jit(cholesky)/cholesky | solution.py:77
  562.4 9.8 %custom-call.36 = f32[1,128,128]{1,2,0:T(8,128)S(1)} custom-call(f32[1,128,128]{2,1,0:T(8,128)S(1)} %get-tuple-element.69), custom_call_target="InvertDiagBlocksLowerTriangular" | custom-call | tf_op jit(solution)/shard_map/jit(cholesky)/cholesky | solution.py:77
  573.6 11.7 %cholesky.377 = f32[128,128]{1,0:T(8,128)S(1)} custom-call(f32[128,128]{1,0:T(8,128)S(1)} %cholesky.443), custom_call_target="Cholesky" | custom-call | tf_op jit(solution)/shard_map/jit(cholesky)/cholesky | solution.py:77
  586.7 10.0 %custom-call.37 = f32[1,128,128]{1,2,0:T(8,128)S(1)} custom-call(f32[1,128,128]{2,1,0:T(8,128)S(1)} %get-tuple-element.66), custom_call_target="InvertDiagBlocksLowerTriangular" | custom-call | tf_op jit(solution)/shard_map/jit(cholesky)/cholesky | solution.py:77
  598.8 13.2 %cholesky.398 = f32[128,128]{1,0:T(8,128)} custom-call(f32[128,128]{1,0:T(8,128)} %cholesky.448), custom_call_target="Cholesky" | custom-call | tf_op jit(solution)/shard_map/jit(cholesky)/cholesky | solution.py:77
  612.0 1.5 select_reduce_fusion.1
  614.2 11.3 %custom-call.38 = f32[1,128,128]{1,2,0:T(8,128)} custom-call(f32[1,128,128]{2,1,0:T(8,128)} %get-tuple-element.63), custom_call_target="InvertDiagBlocksLowerTriangular" | custom-call | tf_op jit(solution)/shard_map/jit(cholesky)/cholesky | solution.py:77
  626.9 11.7 %cholesky.415 = f32[128,128]{1,0:T(8,128)S(1)} custom-call(f32[128,128]{1,0:T(8,128)S(1)} %convolution_subtract_fusion.15), custom_call_target="Cholesky" | custom-call | tf_op jit(solution)/shard_map/jit(cholesky)/cholesky | solution.py:77
  642.2 8.0 while.5
  642.8 1.4 bitcast_dynamic-update-slice_fusion.4
  644.8 1.4 bitcast_dynamic-update-slice_fusion.4
  646.8 1.4 bitcast_dynamic-update-slice_fusion.4
  648.8 1.4 bitcast_dynamic-update-slice_fusion.4
  650.2 39.3 %custom-call.26 = f32[4,128,128]{1,2,0:T(8,128)S(1)} custom-call(f32[4,128,128]{2,1,0:T(8,128)S(1)} %get-tuple-element.20), custom_call_target="InvertDiagBlocksLowerTriangular" | custom-call | tf_op jit(solution)/shard_map/triangular_solve | solution.py:16
  693.7 115.5 %all-reduce.8.cloned.1.call-done = f32[512,1,256]{2,0,1:T(8,128)} async-done(((f32[512,1,256]{2,0,1:T(8,128)}), f32[512,1,256]{2,0,1:T(8,128)}) %all-reduce.8.cloned.1.call-update) | async-done | bytes 524304 | tf_op jit(solution)/shard_map/psum | solution.py:12
  809.2 2.0 fusion.23
  812.5 20.5 %all-gather.12.cloned.1.call-done = f32[512,2,256]{2,0,1:T(8,128)} async-done(((f32[512,1,256]{2,0,1:T(8,128)}), f32[512,2,256]{2,0,1:T(8,128)}) %all-gather.12.cloned.1.call-update) | async-done | bytes 1048592 | tf_op jit(solution)/shard_map/all_gather | solution.py:80
  833.0 1.6 copy.31
  (130 shorter events, 50.0 us)
Async XLA Ops:
  7.2 214.4 %all-gather.14.cloned.1.call-start = ((), (), s32[]{:S(2)}) async-start(), calls=%async_computation.7 | async-start | bytes 4210688 | tf_op jit(solution)/shard_map/all_gather | solution.py:49
  8.6 358.9 %all-gather.8.cloned.1.call-start = ((), (), s32[]{:S(2)}) async-start(), calls=%async_computation.1 | async-start | bytes 1114112 | tf_op jit(solution)/shard_map/all_gather | solution.py:59
  10.3 365.5 %all-gather.16.cloned.1.call-start = ((), (), s32[]{:S(2)}) async-start(), calls=%async_computation.8 | async-start | bytes 1114112 | tf_op jit(solution)/shard_map/all_gather | solution.py:48
  11.9 403.3 %reduce-scatter.2.cloned.1.call-start = ((), (), s32[]{:S(2)}) async-start(), calls=%async_computation.2 | async-start | bytes 1572864 | tf_op jit(solution)/shard_map/reduce_scatter | solution.py:72
  231.2 1.0 copy-start
  372.4 0.7 copy-start.3
  375.8 7.7 copy-start.4
  375.8 7.7 copy-start.9
  382.9 0.7 copy-start.5
  388.7 26.5 %copy-start.7 = (f32[512,1,1,256]{3,2,1,0:T(1,128)S(1)}, f32[512,1,1,256]{3,2,1,0:T(1,128)}, u32[]{:S(2)}) copy-start(f32[512,1,1,256]{3,2,1,0:T(1,128)} %param.8) | copy-start | bytes 1572868
  391.9 95.8 %all-reduce.6.cloned.1.call-start = ((), (), s32[]{:S(2)}) async-start(), calls=%async_computation.3 | async-start | bytes 131072 | tf_op jit(solution)/shard_map/psum | solution.py:12
  416.4 0.8 copy-start.1
  443.3 104.2 %all-gather.10.cloned.1.call-start = ((), (), s32[]{:S(2)}) async-start(), calls=%async_computation.4 | async-start | bytes 1114112 | tf_op jit(solution)/shard_map/all_gather | solution.py:76
  487.7 321.4 %all-reduce.8.cloned.1.call-start = ((), (), s32[]{:S(2)}) async-start(), calls=%async_computation.5 | async-start | bytes 1048576 | tf_op jit(solution)/shard_map/psum | solution.py:12
  572.9 0.7 copy-start.6
  689.6 1.5 copy-start.8
  691.5 143.1 %copy-start.2 = (f32[512,256]{1,0:T(8,128)S(1)}, f32[512,256]{1,0:T(8,128)}, u32[]{:S(2)}) copy-start(f32[512,256]{1,0:T(8,128)} %copy-done.1) | copy-start | bytes 1572868
  693.6 139.4 %all-gather.12.cloned.1.call-start = ((), (), s32[]{:S(2)}) async-start(), calls=%async_computation.6 | async-start | bytes 1572864 | tf_op jit(solution)/shard_map/all_gather | solution.py:80
Sparse Core Ops, SparseCore 0:
  13.1 208.4 all-gather.13
  225.1 59.4 all-gather.7
  287.2 63.2 all-gather.15
  392.0 23.1 reduce-scatter.1
  443.5 44.1 all-reduce.5
  491.0 56.4 all-gather.9
  693.7 115.3 all-reduce.7
  811.2 21.7 all-gather.11
where the time goes:
time: 855 us; the launch traced here: 844 us
  waiting for transfers between devices  472 us (55%)
  other arithmetic  248 us (29%)
  local copies, waits for them, and re-layouts  43.7 us (5%)
  matrix products  33.6 us (4%)
  blocking collectives  25.4 us (3%)
  between operations  20.3 us (2%)
    all_gather x1, waiting for transfers between devices, body(): lax.all_gather(child_block[None, :pivot_count, :pivot_count], ('row', 'co...  209 us
    psum x2, waiting for transfers between devices, spread_2(): return lax.psum(kept, axis)  160 us
    another operation x15, other arithmetic, body(): root_factor = jnp.linalg.cholesky(root_corner)  83.6 us
    another operation x5, other arithmetic, lower_solve(): lax.linalg.triangular_solve(factor, right, left_side=True, lower=True)  79.1 us
    another operation x14, other arithmetic, body(): factor = jnp.linalg.cholesky(corner)  78.6 us
    all_gather x1, waiting for transfers between devices, body(): root_corner = lax.all_gather(pivots, 'col', axis=1, tiled=True)  59.6 us
    all_gather x1, blocking collectives, body(): lax.all_gather(assembled[:pivot_count, :], 'row', axis=0, tiled=True)  25.4 us
    reduce_scatter x1, waiting for transfers between devices, body(): lax.psum_scatter(additions, 'half', scatter_dimension=1, tiled=True)  23.3 us
  transfers between devices with their start and end apart: 8, of which 6 were waited for; matrix products, arithmetic and copies ran while one was open for 19% of the time, Pallas kernels for 0%

commit v1 on v0

--- a/solution.py
+++ b/solution.py
@@ -2,6 +2,7 @@
 import jax.numpy as jnp
 from jax import lax
 from jax.sharding import PartitionSpec as P
+from jax.lax import all_gather
 
 BLK = 128
 PB = 32
@@ -9,7 +10,7 @@
 
 def spread_2(value, axis, source):
     kept = jnp.where(lax.axis_index(axis) == source, value, 0).astype(value.dtype)
-    return lax.psum(kept, axis)
+    return jnp.sum(all_gather(kept, axis_name=axis), 0)
 
 
 def lower_solve(factor, right):

time: 855 us -> 787 us (0.920)
  waiting for transfers between devices: 472 us -> 391 us
  blocking collectives: 25.4 us -> 34.6 us
    psum x2 -> x0, waiting for transfers between devices: 160 us -> none  [spread_2(): return lax.psum(kept, axis)]
    all_gather x0 -> x1, waiting for transfers between devices: none -> 86.9 us  [spread_2(): return jnp.sum(all_gather(kept, axis_name=axis), 0)]
    all_gather x0 -> x1, blocking collectives: none -> 9.2 us  [spread_2(): return jnp.sum(all_gather(kept, axis_name=axis), 0)]
  transfers between devices with their start and end apart: 8 -> 7, of which waited for: 6 -> 5; matrix products, arithmetic and copies ran while one was open for 19% -> 20% of each run, Pallas kernels for 0% -> 0%
where the time goes in v1:
time: 787 us; the launch traced here: 776 us
  waiting for transfers between devices  391 us (50%)
  other arithmetic  248 us (32%)
  local copies, waits for them, and re-layouts  44.8 us (6%)
  matrix products  35.9 us (5%)
  blocking collectives  34.6 us (4%)
  between operations  20.2 us (3%)
    all_gather x1, waiting for transfers between devices, body(): lax.all_gather(child_block[None, :pivot_count, :pivot_count], ('row', 'co...  209 us
    all_gather x1, waiting for transfers between devices, spread_2(): return jnp.sum(all_gather(kept, axis_name=axis), 0)  86.9 us
    another operation x5, other arithmetic, lower_solve(): lax.linalg.triangular_solve(factor, right, left_side=True, lower=True)  80.1 us
    another operation x15, other arithmetic, body(): root_factor = jnp.linalg.cholesky(root_corner)  79.2 us
    another operation x14, other arithmetic, body(): factor = jnp.linalg.cholesky(corner)  78.6 us
    all_gather x1, waiting for transfers between devices, body(): root_corner = lax.all_gather(pivots, 'col', axis=1, tiled=True)  53.4 us
    all_gather x1, blocking collectives, body(): lax.all_gather(assembled[:pivot_count, :], 'row', axis=0, tiled=True)  25.4 us
    reduce_scatter x1, waiting for transfers between devices, body(): lax.psum_scatter(additions, 'half', scatter_dimension=1, tiled=True)  23.3 us
  transfers between devices with their start and end apart: 7, of which 5 were waited for; matrix products, arithmetic and copies ran while one was open for 20% of the time, Pallas kernels for 0%

profile of v1, /device:TPU:1, one launch (start us, length us, event | category | flops | bytes accessed | tf_op | source)
XLA Modules:
  0.0 776.0 jit_solution(6063292462937032915)
XLA Ops:
  10.4 1.5 slice.132
  12.8 208.7 %all-gather.17.cloned.1.call-done = f32[8192,32]{1,0:T(8,128)} async-done(((f32[32,32]{1,0:T(8,128)}), f32[8192,32]{1,0:T(8,128)}) %all-gather.17.cloned.1.call-update) | async-done | bytes 1048592 | tf_op jit(solution)/shard_map/all_gather | solution.py:50
  221.5 5.6 copy.12
  227.1 3.5 reshape.123
  231.3 11.7 %cholesky.286 = f32[128,128]{1,0:T(8,128)S(1)} custom-call(f32[128,128]{1,0:T(8,128)S(1)} %cholesky.426), custom_call_target="Cholesky" | custom-call | tf_op jit(solution)/shard_map/jit(cholesky)/cholesky | solution.py:58
  243.0 9.8 %custom-call.31 = f32[1,128,128]{1,2,0:T(8,128)S(1)} custom-call(f32[1,128,128]{2,1,0:T(8,128)S(1)} %get-tuple-element.74), custom_call_target="InvertDiagBlocksLowerTriangular" | custom-call | tf_op jit(solution)/shard_map/jit(cholesky)/cholesky | solution.py:58
  253.6 11.7 %cholesky.305 = f32[128,128]{1,0:T(8,128)S(1)} custom-call(f32[128,128]{1,0:T(8,128)S(1)} %cholesky.430), custom_call_target="Cholesky" | custom-call | tf_op jit(solution)/shard_map/jit(cholesky)/cholesky | solution.py:58
  265.4 10.0 %custom-call.32 = f32[1,128,128]{1,2,0:T(8,128)S(1)} custom-call(f32[1,128,128]{2,1,0:T(8,128)S(1)} %get-tuple-element.71), custom_call_target="InvertDiagBlocksLowerTriangular" | custom-call | tf_op jit(solution)/shard_map/jit(cholesky)/cholesky | solution.py:58
  276.0 11.7 %cholesky.326 = f32[128,128]{1,0:T(8,128)S(1)} custom-call(f32[128,128]{1,0:T(8,128)S(1)} %cholesky.435), custom_call_target="Cholesky" | custom-call | tf_op jit(solution)/shard_map/jit(cholesky)/cholesky | solution.py:58
  288.5 9.8 %custom-call.33 = f32[1,128,128]{1,2,0:T(8,128)S(1)} custom-call(f32[1,128,128]{2,1,0:T(8,128)S(1)} %get-tuple-element.68), custom_call_target="InvertDiagBlocksLowerTriangular" | custom-call | tf_op jit(solution)/shard_map/jit(cholesky)/cholesky | solution.py:58
  298.9 11.7 %cholesky.343 = f32[128,128]{1,0:T(8,128)S(1)} custom-call(f32[128,128]{1,0:T(8,128)S(1)} %convolution_subtract_fusion.16), custom_call_target="Cholesky" | custom-call | tf_op jit(solution)/shard_map/jit(cholesky)/cholesky | solution.py:58
  314.6 8.9 %while.6 = (s32[]{:T(128)}, f32[512,512]{1,0:T(8,128)S(1)}, s32[4,2]{0,1:T(2,128)S(1)}, f32[4,128,128]{2,1,0:T(8,128)S(1)}, s32[]{:T(128)}) while((s32[]{:T(128)}, f32[512,512]{1,0:T(8,128)S(1)}, s32[4,2]{0,1:T(2,128)S(1)}, f32[4,128,128]{2,1,0:T(8,128)S(1)}, s32[]{:T(128)}) %tuple.62), condition=%wide.while_cond, body=%wide.while_body.sunk | while | flops 2 | bytes 131181 | solution.py:17
  315.7 1.4 bitcast_dynamic-update-slice_fusion.5
  317.9 1.4 bitcast_dynamic-update-slice_fusion.5
  320.0 1.4 bitcast_dynamic-update-slice_fusion.5
  322.1 1.4 bitcast_dynamic-update-slice_fusion.5
  323.5 39.3 %custom-call.34 = f32[4,128,128]{1,2,0:T(8,128)S(1)} custom-call(f32[4,128,128]{2,1,0:T(8,128)S(1)} %get-tuple-element.27), custom_call_target="InvertDiagBlocksLowerTriangular" | custom-call | tf_op jit(solution)/shard_map/triangular_solve/custom-call.3 | solution.py:17
  366.0 1.4 convolution_subtract_fusion.2
  367.8 1.6 convolution_subtract_fusion.6
  369.9 1.4 fusion.39
  373.0 1.4 convolution_subtract_fusion.4
  374.8 1.6 convolution_subtract_fusion.7
  377.5 4.0 convolution_subtract_fusion
  381.6 1.6 reshape.124
  383.1 1.7 fusion.11
  388.1 23.3 %reduce-scatter.2.cloned.1.call-done = f32[512,1,256]{2,0,1:T(8,128)} async-done(((f32[512,2,256]{2,0,1:T(8,128)}), f32[512,1,256]{2,0,1:T(8,128)}) %reduce-scatter.2.cloned.1.call-update) | async-done | bytes 524304 | tf_op jit(solution)/shard_map/reduce_scatter | solution.py:73
  412.6 25.4 %all_gather.31 = f32[512,256]{1,0:T(8,128)S(1)} all-gather(f32[32,256]{1,0:T(8,128)S(1)} %slice.211), channel_id=1, replica_groups=mesh['half'=2,'row'=16,'col'=16] {'row'}, dimensions={0}, use_global_device_ids=true | all-gather | bytes 557056 | tf_op jit(solution)/shard_map/all_gather | solution.py:75
  438.1 9.2 %all-gather.2 = f32[1024,32]{1,0:T(8,128)S(1)} all-gather(f32[512,32]{1,0:T(8,128)S(1)} %slice_select_fusion), channel_id=4, replica_groups=mesh['half'=2,'row'=16,'col'=16] {'half'}, dimensions={0}, use_global_device_ids=true | all-gather | bytes 196608 | tf_op jit(solution)/shard_map/all_gather | solution.py:13
  448.3 53.4 %all-gather.13.cloned.1.call-done = f32[512,512]{0,1:T(8,128)} async-done(((f32[512,32]{0,1:T(8,128)}), f32[512,512]{0,1:T(8,128)}) %all-gather.13.cloned.1.call-update) | async-done | bytes 1048592 | tf_op jit(solution)/shard_map/all_gather | solution.py:77
  501.7 1.6 copy.17
  503.3 1.4 fusion.8
  505.7 11.7 %cholesky.358 = f32[128,128]{1,0:T(8,128)S(1)} custom-call(f32[128,128]{1,0:T(8,128)S(1)} %cholesky.439), custom_call_target="Cholesky" | custom-call | tf_op jit(solution)/shard_map/jit(cholesky)/cholesky | solution.py:78
  517.6 9.8 %custom-call.36 = f32[1,128,128]{1,2,0:T(8,128)S(1)} custom-call(f32[1,128,128]{2,1,0:T(8,128)S(1)} %get-tuple-element.64), custom_call_target="InvertDiagBlocksLowerTriangular" | custom-call | tf_op jit(solution)/shard_map/jit(cholesky)/cholesky | solution.py:78
  529.9 11.7 %cholesky.377 = f32[128,128]{1,0:T(8,128)S(1)} custom-call(f32[128,128]{1,0:T(8,128)S(1)} %cholesky.443), custom_call_target="Cholesky" | custom-call | tf_op jit(solution)/shard_map/jit(cholesky)/cholesky | solution.py:78
  543.1 10.0 %custom-call.37 = f32[1,128,128]{1,2,0:T(8,128)S(1)} custom-call(f32[1,128,128]{2,1,0:T(8,128)S(1)} %get-tuple-element.61), custom_call_target="InvertDiagBlocksLowerTriangular" | custom-call | tf_op jit(solution)/shard_map/jit(cholesky)/cholesky | solution.py:78
  554.6 11.7 %cholesky.398 = f32[128,128]{1,0:T(8,128)S(1)} custom-call(f32[128,128]{1,0:T(8,128)S(1)} %cholesky.448), custom_call_target="Cholesky" | custom-call | tf_op jit(solution)/shard_map/jit(cholesky)/cholesky | solution.py:78
  567.0 9.8 %custom-call.38 = f32[1,128,128]{1,2,0:T(8,128)S(1)} custom-call(f32[1,128,128]{2,1,0:T(8,128)S(1)} %get-tuple-element.58), custom_call_target="InvertDiagBlocksLowerTriangular" | custom-call | tf_op jit(solution)/shard_map/jit(cholesky)/cholesky | solution.py:78
  578.3 11.7 %cholesky.415 = f32[128,128]{1,0:T(8,128)S(1)} custom-call(f32[128,128]{1,0:T(8,128)S(1)} %convolution_subtract_fusion.15), custom_call_target="Cholesky" | custom-call | tf_op jit(solution)/shard_map/jit(cholesky)/cholesky | solution.py:78
  594.6 12.0 %while.5 = (s32[]{:T(128)}, f32[512,512]{1,0:T(8,128)}, s32[4,2]{0,1:T(2,128)S(1)}, f32[4,128,128]{2,1,0:T(8,128)S(1)}, s32[]{:T(128)}) while((s32[]{:T(128)}, f32[512,512]{1,0:T(8,128)}, s32[4,2]{0,1:T(2,128)S(1)}, f32[4,128,128]{2,1,0:T(8,128)S(1)}, s32[]{:T(128)}) %tuple.82), condition=%wide.while_cond.1, body=%wide.while_body.1.sunk | while | flops 2 | bytes 131181 | solution.py:17
  595.2 2.3 bitcast_dynamic-update-slice_fusion.4
  598.3 2.3 bitcast_dynamic-update-slice_fusion.4
  601.3 2.3 bitcast_dynamic-update-slice_fusion.4
  604.3 2.3 bitcast_dynamic-update-slice_fusion.4
  606.6 39.3 %custom-call.26 = f32[4,128,128]{1,2,0:T(8,128)S(1)} custom-call(f32[4,128,128]{2,1,0:T(8,128)S(1)} %get-tuple-element.20), custom_call_target="InvertDiagBlocksLowerTriangular" | custom-call | tf_op jit(solution)/shard_map/triangular_solve | solution.py:17
  651.7 86.9 %all-gather.15.cloned.1.call-done = f32[16,512,256]{2,1,0:T(8,128)} async-done(((f32[1,512,256]{2,1,0:T(8,128)}), f32[16,512,256]{2,1,0:T(8,128)}) %all-gather.15.cloned.1.call-update) | async-done | bytes 8388624 | tf_op jit(solution)/shard_map/all_gather | solution.py:13
  738.7 4.8 reduce_sum.19
  745.9 18.5 %all-gather.21.cloned.1.call-done = f32[512,512]{1,0:T(8,128)} async-done(((f32[512,256]{1,0:T(8,128)}), f32[512,512]{1,0:T(8,128)}) %all-gather.21.cloned.1.call-update) | async-done | bytes 1048592 | tf_op jit(solution)/shard_map/all_gather | solution.py:81
  764.4 3.0 fusion
  (115 shorter events, 47.3 us)
Async XLA Ops:
  7.2 214.4 %all-gather.17.cloned.1.call-start = ((), (), s32[]{:S(2)}) async-start(), calls=%async_computation.5 | async-start | bytes 4210688 | tf_op jit(solution)/shard_map/all_gather | solution.py:50
  8.6 354.3 %all-gather.11.cloned.1.call-start = ((), (), s32[]{:S(2)}) async-start(), calls=%async_computation.1 | async-start | bytes 1114112 | tf_op jit(solution)/shard_map/all_gather | solution.py:60
  10.3 359.5 %all-gather.19.cloned.1.call-start = ((), (), s32[]{:S(2)}) async-start(), calls=%async_computation.6 | async-start | bytes 1114112 | tf_op jit(solution)/shard_map/all_gather | solution.py:49
  11.9 399.4 %reduce-scatter.2.cloned.1.call-start = ((), (), s32[]{:S(2)}) async-start(), calls=%async_computation.2 | async-start | bytes 1572864 | tf_op jit(solution)/shard_map/reduce_scatter | solution.py:73
  376.8 0.7 copy-start.1
  388.0 113.7 %all-gather.13.cloned.1.call-start = ((), (), s32[]{:S(2)}) async-start(), calls=%async_computation.3 | async-start | bytes 1114112 | tf_op jit(solution)/shard_map/all_gather | solution.py:77
  448.1 290.6 %all-gather.15.cloned.1.call-start = ((), (), s32[]{:S(2)}) async-start(), calls=%async_computation.4 | async-start | bytes 8912896 | tf_op jit(solution)/shard_map/all_gather | solution.py:13
  504.7 1.0 copy-start
  651.7 91.8 %copy-start.2 = (f32[128,512]{1,0:T(8,128)S(1)}, f32[128,512]{1,0:T(8,128)}, u32[]{:S(2)}) copy-start(f32[128,512]{1,0:T(8,128)} %copy-done.1) | copy-start | bytes 786436
  651.7 112.7 %all-gather.21.cloned.1.call-start = ((), (), s32[]{:S(2)}) async-start(), calls=%async_computation.7 | async-start | bytes 1572864 | tf_op jit(solution)/shard_map/all_gather | solution.py:81
Sparse Core Ops, SparseCore 0:
  13.1 208.4 all-gather.16
  225.1 59.6 all-gather.10
  287.5 62.4 all-gather.18
  388.1 23.1 reduce-scatter.1
  448.2 53.4 all-gather.12
  651.8 86.8 all-gather.14
  743.6 20.7 all-gather.20
